TPU v7x, 256 devices: a whole 4x4x8 slice. The times are simulated.
256 devices in a mesh: expert: 16 (over x_hi, y, core), blk: 16 (over x_lo, z).
Axes of the slice: x: 4 (x_hi: 2, x_lo: 2; x = x_hi * 2 + x_lo), y: 4, z: 8, core: 2. Of those that a mesh axis runs over, the one named last changes fastest.
Arguments:
- tokens: bfloat16 [2048, 6144], P(('expert', 'blk')), may hold values from -6 to 6
- out_grad: bfloat16 [2048, 6144], P(('expert', 'blk')), may hold values from -6 to 6
- expert_ids: int32 [2048, 4], P(('expert', 'blk')), may hold values from 0 to 15, as said below
- slots: int32 [2048, 4], P(('expert', 'blk')), may hold values from 0 to 2, as said below
- gates: bfloat16 [2048, 4], P(('expert', 'blk')), may hold values from 0.099609375 to 0.59765625
- w_in: bfloat16 [16, 5376, 6144], P('expert', 'blk'), may hold values from -0.078125 to 0.078125
- w_down: bfloat16 [16, 5376, 6144], P('expert', 'blk'), may hold values from -0.078125 to 0.078125
Outputs:
- grad_tokens: bfloat16 [2048, 6144], P(('expert', 'blk'))
- grad_gates: bfloat16 [2048, 4], P(('expert', 'blk'))
Inputs may be any that keep to these rules, and one draw needn't show every extreme that they name: `expert_ids`: within the 8 tokens of one device, a token names 4 different experts, no expert is named more than 3 times, and one expert is named exactly 3 times by every device. Among the entries of one device that name one expert, the slots are 0 to their count minus 1, each once.
All inputs are finite; a program needn't handle non-finite values.
Results may differ from a plain program's by a relative error of at most 0.019.
Values may be sent and summed in bfloat16 or wider, within the bound.
A program may use at most 128 MiB of HBM per device.

v0:
```python
import jax
import jax.numpy as jnp
from jax import lax
from jax.sharding import PartitionSpec as P


def hidden_terms(rows_x, rows_dy, rows_gate, weight_in, weight_down):
    contract = (((1,), (1,)), ((), ()))
    pre = lax.dot_general(rows_x, weight_in, contract, preferred_element_type=jnp.float32)
    back = lax.dot_general(rows_dy, weight_down, contract, preferred_element_type=jnp.float32)
    sigma = jax.nn.sigmoid(pre)
    gate_part = jnp.sum(pre * sigma * back, axis=1)
    slope = rows_gate.astype(jnp.float32)[:, None] * back * sigma * (1.0 + pre * (1.0 - sigma))
    return (slope.astype(jnp.bfloat16), gate_part)


def per_device(tokens, out_grad, expert_ids, slots, gates, w_in, w_down):
    tok_count = tokens.shape[0]
    top_count = expert_ids.shape[1]
    expert_count = lax.axis_size("expert")
    capacity = max(2, (tok_count * top_count + expert_count - 1) // expert_count + 1)
    slot_count = expert_count * capacity
    target = expert_ids * capacity + slots
    matches = (target[None, :, :] == jnp.arange(slot_count, dtype=jnp.int32)[:, None, None]).astype(
        jnp.float32
    )
    placing = jnp.sum(matches, axis=2).astype(jnp.bfloat16)
    send_x = jnp.dot(placing, tokens, preferred_element_type=jnp.float32).astype(jnp.bfloat16)
    send_dy = jnp.dot(placing, out_grad, preferred_element_type=jnp.float32).astype(jnp.bfloat16)
    send_gate = jnp.einsum("stk,tk->s", matches, gates.astype(jnp.float32)).astype(jnp.bfloat16)
    recv_x, recv_dy, recv_gate = (
        lax.all_to_all(send_x, "expert", split_axis=0, concat_axis=0, tiled=True),
        lax.all_to_all(send_dy, "expert", split_axis=0, concat_axis=0, tiled=True),
        lax.all_to_all(send_gate, "expert", split_axis=0, concat_axis=0, tiled=True),
    )
    weight_in = w_in[0]
    weight_down = w_down[0]
    all_x, all_dy, all_gate = (
        lax.all_gather(recv_x, "blk", axis=0, tiled=True),
        lax.all_gather(recv_dy, "blk", axis=0, tiled=True),
        lax.all_gather(recv_gate, "blk", axis=0, tiled=True),
    )
    slope, gate_part = hidden_terms(all_x, all_dy, all_gate, weight_in, weight_down)
    grad_rows = lax.psum_scatter(
        jnp.dot(slope, weight_in, preferred_element_type=jnp.float32).astype(jnp.bfloat16),
        "blk",
        scatter_dimension=0,
        tiled=True,
    )
    gate_rows = lax.psum_scatter(gate_part, "blk", scatter_dimension=0, tiled=True)
    back_rows, back_gate = (
        lax.all_to_all(grad_rows, "expert", split_axis=0, concat_axis=0, tiled=True),
        lax.all_to_all(
            gate_rows.astype(jnp.bfloat16), "expert", split_axis=0, concat_axis=0, tiled=True
        ),
    )
    grad_tokens = lax.dot_general(
        placing, back_rows, (((0,), (0,)), ((), ())), preferred_element_type=jnp.float32
    ).astype(jnp.bfloat16)
    grad_gates = jnp.einsum("stk,s->tk", matches, back_gate.astype(jnp.float32)).astype(
        jnp.bfloat16
    )
    return (grad_tokens, grad_gates)


def solution(mesh):
    return jax.shard_map(
        per_device,
        mesh=mesh,
        in_specs=(
            P(("expert", "blk"), None),
            P(("expert", "blk"), None),
            P(("expert", "blk"), None),
            P(("expert", "blk"), None),
            P(("expert", "blk"), None),
            P("expert", "blk", None),
            P("expert", "blk", None),
        ),
        out_specs=(P(("expert", "blk"), None), P(("expert", "blk"), None)),
        check_vma=False,
    )
```

profile of v0, /device:TPU:1, one launch (start us, length us, event | category | flops | bytes accessed | tf_op | source)
XLA Modules:
  0.0 417.5 jit_solution(10140539445193351380)
XLA Ops:
  7.2 0.7 multiply_add_fusion
  8.1 0.3 convolution_convert_fusion.1
  8.4 0.4 all_to_all.46
  8.8 22.5 %all_to_all.62 = bf16[16,3,6144]{2,1,0:T(4,128)(2,1)S(1)} all-to-all(bf16[16,3,6144]{2,1,0:T(4,128)(2,1)S(1)} %all_to_all.46), channel_id=1, replica_groups=mesh['expert'=16,'blk'=16] {'expert'}, dimensions={0} | all-to-all | bytes 1179648 | tf_op jit(solution)/shard_map/all_to_all | solution.py:32
  31.4 1.2 all_to_all.48
  32.7 0.3 convolution_convert_fusion.2
  33.0 0.4 all_to_all.43
  33.4 17.8 %all_to_all.63 = bf16[16,3,6144]{2,1,0:T(4,128)(2,1)S(1)} all-to-all(bf16[16,3,6144]{2,1,0:T(4,128)(2,1)S(1)} %all_to_all.43), channel_id=1, replica_groups=mesh['expert'=16,'blk'=16] {'expert'}, dimensions={0} | all-to-all | bytes 1179648 | tf_op jit(solution)/shard_map/all_to_all | solution.py:33
  51.2 1.2 all_to_all.45
  52.5 0.2 fusion.5
  52.7 0.7 all_to_all.55
  53.4 99.0 %all-to-all-start = ((bf16[16,3,1]{1,2,0:T(2,128)(2,1)}), bf16[16,3,1]{1,2,0:T(2,128)(2,1)S(1)}, u32[]{:S(2)}, u32[]{:S(2)}) async-start(bf16[16,3,1]{1,2,0:T(2,128)(2,1)} %all_to_all.55), calls=%async_computation | async-start | bytes 16384 | tf_op jit(solution)/shard_map/all_to_all | solution.py:34
  152.5 0.6 fusion.16
  153.6 5.8 %all-to-all-done = bf16[16,3,1]{1,2,0:T(2,128)(2,1)S(1)} async-done(((bf16[16,3,1]{1,2,0:T(2,128)(2,1)}), bf16[16,3,1]{1,2,0:T(2,128)(2,1)S(1)}, u32[]{:S(2)}, u32[]{:S(2)}) %all-to-all-start) | async-done | bytes 128 | tf_op jit(solution)/shard_map/all_to_all | solution.py:34
  159.4 0.1 reshape.16
  159.6 0.2 dynamic-update-slice
  159.8 32.6 %all-reduce = bf16[768]{0:T(1024)(128)(2,1)S(1)} all-reduce(bf16[768]{0:T(1024)(128)(2,1)S(1)} %dynamic-update-slice), channel_id=1, replica_groups=mesh['expert'=16,'blk'=16] {'blk'}, use_global_device_ids=true, to_apply=%add | all-reduce | flops 768 | bytes 3072
  192.4 11.0 %fusion.1 = f32[768,336]{0,1:T(8,128)S(1)} fusion(bf16[768,6144]{1,0:T(8,128)(2,1)} %all-gather.5.cloned.1.call-done, bf16[1,336,6144]{2,1,0:T(8,128)(2,1)} %param.12), kind=kOutput, calls=%fused_computation.5 | convolution fusion | flops 3170893824 | bytes 14598144 | tf_op jit(solution)/shard_map/dot_general | solution.py:9
  203.4 53.5 %all-gather.3.cloned.1.call-done = bf16[768,6144]{1,0:T(8,128)(2,1)} async-done(((bf16[48,6144]{1,0:T(8,128)(2,1)}), bf16[768,6144]{1,0:T(8,128)(2,1)}) %all-gather.3.cloned.1.call-update) | async-done | bytes 9437200 | tf_op jit(solution)/shard_map/all_gather | solution.py:40
  257.0 11.0 %multiply_reduce_fusion = (f32[768]{0:T(1024)S(1)}, f32[768,336]{0,1:T(8,128)S(1)}) fusion(f32[768,336]{0,1:T(8,128)S(1)} %fusion.1, bf16[768,6144]{1,0:T(8,128)(2,1)} %all-gather.3.cloned.1.call-done, bf16[1,336,6144]{2,1,0:T(8,128)(2,1)} %param.13), kind=kOutput, calls=%fused_computation.11 | convolution fusion | flops 3172441344 | bytes 15633408 | tf_op jit(solution)/shard_map/dot_general | solution.py:10
  268.0 8.0 %convolution_convert_fusion = bf16[768,6144]{1,0:T(8,128)(2,1)} fusion(bf16[1,336,6144]{2,1,0:T(8,128)(2,1)S(1)} %copy-done.1, f32[768,336]{0,1:T(8,128)S(1)} %fusion.1, f32[768,336]{0,1:T(8,128)S(1)} %get-tuple-element.5, f32[768]{0:T(1024)S(1)} %convert_element_type.38), kind=kOutput, calls=%fused_computation | convolution fusion | flops 3178192896 | bytes 15633408 | tf_op jit(solution)/shard_map/dot_general | solution.py:45
  276.7 27.5 %all-reduce.1 = bf16[768]{0:T(1024)(128)(2,1)S(1)} all-reduce(f32[768]{0:T(1024)S(1)} %get-tuple-element.4), channel_id=3, replica_groups=mesh['expert'=16,'blk'=16] {'blk'}, use_global_device_ids=true, to_apply=%region_3.0.clone | all-reduce | flops 768 | bytes 4608
  304.3 0.7 all_to_all.56
  305.0 12.2 %all-to-all-start.4 = ((bf16[16,3,1]{1,2,0:T(2,128)(2,1)}), bf16[16,3,1]{1,2,0:T(2,128)(2,1)S(1)}, u32[]{:S(2)}, u32[]{:S(2)}) async-start(bf16[16,3,1]{1,2,0:T(2,128)(2,1)} %all_to_all.56), calls=%async_computation.5 | async-start | bytes 16384 | tf_op jit(solution)/shard_map/all_to_all | solution.py:53
  317.2 68.8 %reduce-scatter.2.cloned.1.call-done = bf16[48,6144]{1,0:T(8,128)(2,1)} async-done(((bf16[768,6144]{1,0:T(8,128)(2,1)}), bf16[48,6144]{1,0:T(8,128)(2,1)}) %reduce-scatter.2.cloned.1.call-update) | async-done | bytes 589840 | tf_op jit(solution)/shard_map/reduce_scatter | solution.py:44
  386.0 2.1 all_to_all.49
  388.1 7.1 %all-to-all-start.3 = ((bf16[16,3,6144]{2,1,0:T(4,128)(2,1)}), bf16[16,3,6144]{2,1,0:T(4,128)(2,1)S(1)}, u32[]{:S(2)}, u32[]{:S(2)}) async-start(bf16[16,3,6144]{2,1,0:T(4,128)(2,1)} %all_to_all.49), calls=%async_computation.4 | async-start | bytes 1572864 | tf_op jit(solution)/shard_map/all_to_all | solution.py:52
  395.3 0.2 fusion.8
  395.5 0.6 convert_element_type.45
  396.1 13.5 %all-to-all-done.3 = bf16[16,3,6144]{2,1,0:T(4,128)(2,1)S(1)} async-done(((bf16[16,3,6144]{2,1,0:T(4,128)(2,1)}), bf16[16,3,6144]{2,1,0:T(4,128)(2,1)S(1)}, u32[]{:S(2)}, u32[]{:S(2)}) %all-to-all-start.3) | async-done | bytes 589856 | tf_op jit(solution)/shard_map/all_to_all | solution.py:52
  409.6 0.5 all_to_all.51
  410.1 0.8 convolution_convert_fusion.3
  (25 shorter events, 0.5 us)
Async XLA Ops:
  7.2 0.9 copy-start
  7.2 25.5 %copy-start.2 = (bf16[8,6144]{1,0:T(8,128)(2,1)S(1)}, bf16[8,6144]{1,0:T(8,128)(2,1)}, u32[]{:S(2)}) copy-start(bf16[8,6144]{1,0:T(8,128)(2,1)} %param.8) | copy-start | bytes 294916
  7.2 185.2 %all-gather.5.cloned.1.call-start = ((), (), s32[]{:S(2)}) async-start(), calls=%async_computation.7 | async-start | bytes 10027008 | tf_op jit(solution)/shard_map/all_gather | solution.py:39
  31.4 21.1 %copy-start.4 = (bf16[8,4]{0,1:T(4,128)(2,1)S(1)}, bf16[8,4]{0,1:T(4,128)(2,1)}, u32[]{:S(2)}) copy-start(bf16[8,4]{0,1:T(4,128)(2,1)} %param.11) | copy-start | bytes 196
  31.4 121.1 %copy-start.3 = (u32[256]{0:T(256)S(1)}, u32[256]{0:T(256)}, u32[]{:S(2)}) copy-start(u32[256]{0:T(256)} %constant.15) | copy-start | bytes 3076
  32.6 224.3 %all-gather.3.cloned.1.call-start = ((), (), s32[]{:S(2)}) async-start(), calls=%async_computation.6 | async-start | bytes 10027008 | tf_op jit(solution)/shard_map/all_gather | solution.py:40
  53.4 106.0 %all-to-all-start = ((bf16[16,3,1]{1,2,0:T(2,128)(2,1)}), bf16[16,3,1]{1,2,0:T(2,128)(2,1)S(1)}, u32[]{:S(2)}, u32[]{:S(2)}) async-start(bf16[16,3,1]{1,2,0:T(2,128)(2,1)} %all_to_all.55), calls=%async_computation | async-start | bytes 16384 | tf_op jit(solution)/shard_map/all_to_all | solution.py:34
  152.4 233.6 %reduce-scatter.2.cloned.1.call-start = ((), (), s32[]{:S(2)}) async-start(), calls=%async_computation.8 | async-start | bytes 10027008 | tf_op jit(solution)/shard_map/reduce_scatter | solution.py:44
  257.0 11.0 %copy-start.1 = (bf16[1,336,6144]{2,1,0:T(8,128)(2,1)S(1)}, bf16[1,336,6144]{2,1,0:T(8,128)(2,1)}, u32[]{:S(2)}) copy-start(bf16[1,336,6144]{2,1,0:T(8,128)(2,1)} %param.12) | copy-start | bytes 12386308
  305.0 83.1 %all-to-all-start.4 = ((bf16[16,3,1]{1,2,0:T(2,128)(2,1)}), bf16[16,3,1]{1,2,0:T(2,128)(2,1)S(1)}, u32[]{:S(2)}, u32[]{:S(2)}) async-start(bf16[16,3,1]{1,2,0:T(2,128)(2,1)} %all_to_all.56), calls=%async_computation.5 | async-start | bytes 16384 | tf_op jit(solution)/shard_map/all_to_all | solution.py:53
  388.1 21.5 %all-to-all-start.3 = ((bf16[16,3,6144]{2,1,0:T(4,128)(2,1)}), bf16[16,3,6144]{2,1,0:T(4,128)(2,1)S(1)}, u32[]{:S(2)}, u32[]{:S(2)}) async-start(bf16[16,3,6144]{2,1,0:T(4,128)(2,1)} %all_to_all.49), calls=%async_computation.4 | async-start | bytes 1572864 | tf_op jit(solution)/shard_map/all_to_all | solution.py:52
Sparse Core Ops, SparseCore 0:
  32.7 110.5 all-gather.4
  145.1 111.8 all-gather.2
  276.2 109.7 reduce-scatter.1
where the time goes:
time: 418 us; the launch traced here: 417 us
  waiting for transfers between devices  142 us (34%)
  starting transfers between devices  118 us (28%)
  blocking collectives  100 us (24%)
  matrix products  32 us (8%)
  between operations  15.1 us (4%)
  local copies, waits for them, and re-layouts  8.4 us (2%)
    all_to_all x1, starting transfers between devices, per_device(): lax.all_to_all(send_gate, 'expert', split_axis=0, concat_axis=0, tiled=True)  99 us
    reduce_scatter x1, waiting for transfers between devices, per_device(): lax.psum_scatter(jnp.dot(slope, weight_in, preferred_element_type=jnp.flo...  68.8 us
    unnamed x2, blocking collectives  60.1 us
    all_gather x1, waiting for transfers between devices, per_device(): lax.all_gather(recv_dy, 'blk', axis=0, tiled=True)  53.5 us
    all_to_all x1, blocking collectives, per_device(): lax.all_to_all(send_x, 'expert', split_axis=0, concat_axis=0, tiled=True)  22.5 us
    all_to_all x1, blocking collectives, per_device(): lax.all_to_all(send_dy, 'expert', split_axis=0, concat_axis=0, tiled=True)  17.8 us
    all_to_all x1, waiting for transfers between devices, per_device(): lax.all_to_all(grad_rows, 'expert', split_axis=0, concat_axis=0, tiled=True)  13.5 us
    all_to_all x1, starting transfers between devices, per_device(): lax.all_to_all(gate_rows.astype(jnp.bfloat16), 'expert', split_axis=0, co...  12.2 us
  transfers between devices with their start and end apart: 6, of which 4 were waited for; matrix products, arithmetic and copies ran while one was open for 3% of the time, Pallas kernels for 0%

commit v1 on v0

--- a/solution.py
+++ b/solution.py
@@ -37,7 +37,9 @@
     weight_down = w_down[0]
     all_x, all_dy, all_gate = (
         lax.all_gather(recv_x, "blk", axis=0, tiled=True),
-        lax.all_gather(recv_dy, "blk", axis=0, tiled=True),
+        jnp.concatenate(
+            lax.all_to_all(jnp.stack([recv_dy] * lax.axis_size("blk")), "blk", 0, 0), axis=0
+        ),
         lax.all_gather(recv_gate, "blk", axis=0, tiled=True),
     )
     slope, gate_part = hidden_terms(all_x, all_dy, all_gate, weight_in, weight_down)

time: 418 us -> 583 us (1.39)
  blocking collectives: 100 us -> 282 us
  starting transfers between devices: 118 us -> 39.3 us
  waiting for transfers between devices: 142 us -> 199 us
    unnamed x2, blocking collectives: 60.1 us -> 259 us
    all_to_all x0 -> x2, waiting for transfers between devices: none -> 108 us  [the longest x1 108 us: per_device(): lax.all_to_all(send_dy, 'expert', split_axis=0, concat_axis=0, tiled=True)]
    all_to_all x1, starting transfers between devices: 99 us -> 4.13 us  [per_device(): lax.all_to_all(send_gate, 'expert', split_axis=0, concat_axis=0, tiled=True)]
    all_gather x1 -> x0, waiting for transfers between devices: 53.5 us -> none  [per_device(): lax.all_gather(recv_dy, 'blk', axis=0, tiled=True)]
    all_to_all x1 -> x0, blocking collectives: 17.8 us -> none  [per_device(): lax.all_to_all(send_dy, 'expert', split_axis=0, concat_axis=0, tiled=True)]
    all_to_all x0 -> x2, starting transfers between devices: none -> 11.6 us  [the longest x1 7.17 us: per_device(): lax.all_to_all(jnp.stack([recv_dy] * lax.axis_size('blk')), 'blk', 0, 0)]
  transfers between devices with their start and end apart: 6 -> 7, of which waited for: 4 -> 4; matrix products, arithmetic and copies ran while one was open for 3% -> 3% of each run, Pallas kernels for 0% -> 0%
where the time goes in v1:
time: 583 us
  blocking collectives  282 us (48%)
  waiting for transfers between devices  199 us (34%)
  starting transfers between devices  39.3 us (7%)
  matrix products  31.8 us (5%)
  between operations  15.5 us (3%)
  local copies, waits for them, and re-layouts  13.4 us (2%)
    unnamed x2, blocking collectives  259 us
    all_to_all x1, waiting for transfers between devices, per_device(): lax.all_to_all(send_dy, 'expert', split_axis=0, concat_axis=0, tiled=True)  108 us
    reduce_scatter x1, waiting for transfers between devices, per_device(): lax.psum_scatter(jnp.dot(slope, weight_in, preferred_element_type=jnp.flo...  70.9 us
    all_to_all x1, blocking collectives, per_device(): lax.all_to_all(send_x, 'expert', split_axis=0, concat_axis=0, tiled=True)  22.5 us
    all_to_all x1, starting transfers between devices, per_device(): lax.all_to_all(gate_rows.astype(jnp.bfloat16), 'expert', split_axis=0, co...  16.6 us
    all_to_all x1, waiting for transfers between devices, per_device(): lax.all_to_all(grad_rows, 'expert', split_axis=0, concat_axis=0, tiled=True)  13.5 us
  transfers between devices with their start and end apart: 7, of which 4 were waited for; matrix products, arithmetic and copies ran while one was open for 3% of the time, Pallas kernels for 0%

profile of v1, /device:TPU:1, one launch (start us, length us, event | category | flops | bytes accessed | tf_op | source)
XLA Modules:
  0.0 582.6 jit_solution(15878380188504523434)
XLA Ops:
  7.2 0.7 multiply_add_fusion
  8.1 0.3 convolution_convert_fusion.1
  8.4 0.4 all_to_all.47
  8.8 22.5 %all_to_all.64 = bf16[16,3,6144]{2,1,0:T(4,128)(2,1)S(1)} all-to-all(bf16[16,3,6144]{2,1,0:T(4,128)(2,1)S(1)} %all_to_all.47), channel_id=1, replica_groups=mesh['expert'=16,'blk'=16] {'expert'}, dimensions={0} | all-to-all | bytes 1179648 | tf_op jit(solution)/shard_map/all_to_all | solution.py:32
  31.4 1.2 all_to_all.49
  32.6 0.3 convolution_convert_fusion.2
  33.0 1.1 all_to_all.44
  34.1 4.4 all-to-all-start.1
  38.7 0.7 all_to_all.56
  39.4 108.4 %all-to-all-done.1 = bf16[16,3,6144]{2,1,0:T(4,128)(2,1)S(1)} async-done(((bf16[16,3,6144]{2,1,0:T(4,128)(2,1)}), bf16[16,3,6144]{2,1,0:T(4,128)(2,1)S(1)}, u32[]{:S(2)}, u32[]{:S(2)}) %all-to-all-start.1) | async-done | bytes 589856 | tf_op jit(solution)/shard_map/all_to_all | solution.py:33
  147.8 4.1 all-to-all-start
  151.9 0.5 stack.4
  152.5 6.5 %all-to-all-done = bf16[16,3,1]{1,2,0:T(2,128)(2,1)S(1)} async-done(((bf16[16,3,1]{1,2,0:T(2,128)(2,1)}), bf16[16,3,1]{1,2,0:T(2,128)(2,1)S(1)}, u32[]{:S(2)}, u32[]{:S(2)}) %all-to-all-start) | async-done | bytes 128 | tf_op jit(solution)/shard_map/all_to_all | solution.py:34
  158.9 4.9 stack.5
  163.8 7.2 %all-to-all-start.2 = ((bf16[16,48,6144]{2,1,0:T(8,128)(2,1)}), bf16[16,48,6144]{2,1,0:T(8,128)(2,1)}, u32[]{:S(2)}, u32[]{:S(2)}) async-start(bf16[16,48,6144]{2,1,0:T(8,128)(2,1)} %stack.5), calls=%async_computation.2 | async-start | bytes 18874368 | tf_op jit(solution)/shard_map/all_to_all | solution.py:41
  171.1 0.6 fusion.16
  172.5 0.2 dynamic-update-slice
  172.7 234.2 %all-reduce = bf16[768]{0:T(1024)(128)(2,1)S(1)} all-reduce(bf16[768]{0:T(1024)(128)(2,1)S(1)} %dynamic-update-slice), channel_id=1, replica_groups=mesh['expert'=16,'blk'=16] {'blk'}, use_global_device_ids=true, to_apply=%add | all-reduce | flops 768 | bytes 3072
  406.9 10.9 %fusion.1 = f32[768,336]{0,1:T(8,128)S(1)} fusion(bf16[768,6144]{1,0:T(8,128)(2,1)} %all-gather.2.cloned.1.call-done, bf16[1,336,6144]{2,1,0:T(8,128)(2,1)} %param.12), kind=kOutput, calls=%fused_computation.5 | convolution fusion | flops 3170893824 | bytes 14598144 | tf_op jit(solution)/shard_map/dot_general | solution.py:9
  417.8 11.0 %multiply_reduce_fusion = (f32[768]{0:T(1024)S(1)}, f32[768,336]{0,1:T(8,128)S(1)}) fusion(f32[768,336]{0,1:T(8,128)S(1)} %fusion.1, bf16[768,6144]{1,0:T(8,128)(2,1)} %bitcast.3, bf16[1,336,6144]{2,1,0:T(8,128)(2,1)} %param.13), kind=kOutput, calls=%fused_computation.11 | convolution fusion | flops 3172441344 | bytes 15633408 | tf_op jit(solution)/shard_map/dot_general | solution.py:10
  428.8 8.0 %convolution_convert_fusion = bf16[768,6144]{1,0:T(8,128)(2,1)} fusion(bf16[1,336,6144]{2,1,0:T(8,128)(2,1)S(1)} %copy-done.1, f32[768,336]{0,1:T(8,128)S(1)} %fusion.1, f32[768,336]{0,1:T(8,128)S(1)} %get-tuple-element.5, f32[768]{0:T(1024)S(1)} %convert_element_type.38), kind=kOutput, calls=%fused_computation | convolution fusion | flops 3178192896 | bytes 15633408 | tf_op jit(solution)/shard_map/dot_general | solution.py:47
  437.5 25.1 %all-reduce.1 = bf16[768]{0:T(1024)(128)(2,1)S(1)} all-reduce(f32[768]{0:T(1024)S(1)} %get-tuple-element.4), channel_id=3, replica_groups=mesh['expert'=16,'blk'=16] {'blk'}, use_global_device_ids=true, to_apply=%region_3.0.clone | all-reduce | flops 768 | bytes 4608
  462.7 0.7 all_to_all.57
  463.4 16.6 %all-to-all-start.5 = ((bf16[16,3,1]{1,2,0:T(2,128)(2,1)}), bf16[16,3,1]{1,2,0:T(2,128)(2,1)S(1)}, u32[]{:S(2)}, u32[]{:S(2)}) async-start(bf16[16,3,1]{1,2,0:T(2,128)(2,1)} %all_to_all.57), calls=%async_computation.6 | async-start | bytes 16384 | tf_op jit(solution)/shard_map/all_to_all | solution.py:55
  480.0 70.9 %reduce-scatter.2.cloned.1.call-done = bf16[48,6144]{1,0:T(8,128)(2,1)} async-done(((bf16[768,6144]{1,0:T(8,128)(2,1)}), bf16[48,6144]{1,0:T(8,128)(2,1)}) %reduce-scatter.2.cloned.1.call-update) | async-done | bytes 589840 | tf_op jit(solution)/shard_map/reduce_scatter | solution.py:46
  551.0 2.1 all_to_all.50
  553.0 6.9 %all-to-all-start.4 = ((bf16[16,3,6144]{2,1,0:T(4,128)(2,1)}), bf16[16,3,6144]{2,1,0:T(4,128)(2,1)S(1)}, u32[]{:S(2)}, u32[]{:S(2)}) async-start(bf16[16,3,6144]{2,1,0:T(4,128)(2,1)} %all_to_all.50), calls=%async_computation.5 | async-start | bytes 1572864 | tf_op jit(solution)/shard_map/all_to_all | solution.py:54
  560.1 0.2 fusion.8
  560.3 0.6 convert_element_type.45
  560.9 13.5 %all-to-all-done.4 = bf16[16,3,6144]{2,1,0:T(4,128)(2,1)S(1)} async-done(((bf16[16,3,6144]{2,1,0:T(4,128)(2,1)}), bf16[16,3,6144]{2,1,0:T(4,128)(2,1)S(1)}, u32[]{:S(2)}, u32[]{:S(2)}) %all-to-all-start.4) | async-done | bytes 589856 | tf_op jit(solution)/shard_map/all_to_all | solution.py:54
  574.4 0.5 all_to_all.52
  574.9 0.8 convolution_convert_fusion.3
  (26 shorter events, 0.8 us)
Async XLA Ops:
  7.2 0.9 copy-start
  7.2 25.4 %copy-start.2 = (bf16[8,6144]{1,0:T(8,128)(2,1)S(1)}, bf16[8,6144]{1,0:T(8,128)(2,1)}, u32[]{:S(2)}) copy-start(bf16[8,6144]{1,0:T(8,128)(2,1)} %param.8) | copy-start | bytes 294916
  7.2 399.7 %all-gather.2.cloned.1.call-start = ((), (), s32[]{:S(2)}) async-start(), calls=%async_computation.7 | async-start | bytes 10027008 | tf_op jit(solution)/shard_map/all_gather | solution.py:39
  8.4 30.1 %copy-start.4 = (bf16[8,4]{0,1:T(4,128)(2,1)S(1)}, bf16[8,4]{0,1:T(4,128)(2,1)}, u32[]{:S(2)}) copy-start(bf16[8,4]{0,1:T(4,128)(2,1)} %param.11) | copy-start | bytes 196
  34.1 113.7 %all-to-all-start.1 = ((bf16[16,3,6144]{2,1,0:T(4,128)(2,1)}), bf16[16,3,6144]{2,1,0:T(4,128)(2,1)S(1)}, u32[]{:S(2)}, u32[]{:S(2)}) async-start(bf16[16,3,6144]{2,1,0:T(4,128)(2,1)} %all_to_all.44), calls=%async_computation.1 | async-start | bytes 1572864 | tf_op jit(solution)/shard_map/all_to_all | solution.py:33
  147.8 11.1 %all-to-all-start = ((bf16[16,3,1]{1,2,0:T(2,128)(2,1)}), bf16[16,3,1]{1,2,0:T(2,128)(2,1)S(1)}, u32[]{:S(2)}, u32[]{:S(2)}) async-start(bf16[16,3,1]{1,2,0:T(2,128)(2,1)} %all_to_all.56), calls=%async_computation | async-start | bytes 16384 | tf_op jit(solution)/shard_map/all_to_all | solution.py:34
  163.8 7.2 %copy-start.3 = (u32[256]{0:T(256)S(1)}, u32[256]{0:T(256)}, u32[]{:S(2)}) copy-start(u32[256]{0:T(256)} %constant.15) | copy-start | bytes 3076
  163.8 253.9 %all-to-all-start.2 = ((bf16[16,48,6144]{2,1,0:T(8,128)(2,1)}), bf16[16,48,6144]{2,1,0:T(8,128)(2,1)}, u32[]{:S(2)}, u32[]{:S(2)}) async-start(bf16[16,48,6144]{2,1,0:T(8,128)(2,1)} %stack.5), calls=%async_computation.2 | async-start | bytes 18874368 | tf_op jit(solution)/shard_map/all_to_all | solution.py:41
  171.0 380.0 %reduce-scatter.2.cloned.1.call-start = ((), (), s32[]{:S(2)}) async-start(), calls=%async_computation.8 | async-start | bytes 10027008 | tf_op jit(solution)/shard_map/reduce_scatter | solution.py:46
  417.8 11.1 %copy-start.1 = (bf16[1,336,6144]{2,1,0:T(8,128)(2,1)S(1)}, bf16[1,336,6144]{2,1,0:T(8,128)(2,1)}, u32[]{:S(2)}) copy-start(bf16[1,336,6144]{2,1,0:T(8,128)(2,1)} %param.12) | copy-start | bytes 12386308
  463.4 89.6 %all-to-all-start.5 = ((bf16[16,3,1]{1,2,0:T(2,128)(2,1)}), bf16[16,3,1]{1,2,0:T(2,128)(2,1)S(1)}, u32[]{:S(2)}, u32[]{:S(2)}) async-start(bf16[16,3,1]{1,2,0:T(2,128)(2,1)} %all_to_all.57), calls=%async_computation.6 | async-start | bytes 16384 | tf_op jit(solution)/shard_map/all_to_all | solution.py:55
  553.0 21.3 %all-to-all-start.4 = ((bf16[16,3,6144]{2,1,0:T(4,128)(2,1)}), bf16[16,3,6144]{2,1,0:T(4,128)(2,1)S(1)}, u32[]{:S(2)}, u32[]{:S(2)}) async-start(bf16[16,3,6144]{2,1,0:T(4,128)(2,1)} %all_to_all.50), calls=%async_computation.5 | async-start | bytes 1572864 | tf_op jit(solution)/shard_map/all_to_all | solution.py:54
Sparse Core Ops, SparseCore 0:
  32.7 110.5 all-gather.1
  437.0 113.9 reduce-scatter.1
